TPU v7x, 512 devices: a whole 4x8x8 slice. The times are simulated.
512 devices in a mesh: aux: 8 (over x, core), ao: 64 (over y, z).
Axes of the slice: x: 4, y: 8, z: 8, core: 2. Of those that a mesh axis runs over, the one named last changes fastest.
Arguments:
- tiles: bfloat16 [64, 768, 4096], P('aux', 'ao'), may hold values from -6 to 6
- slot_row_block: int32 [8, 768], P('aux', 'ao'), may hold values from 0 to 9
- tile_col: int32 [8, 768], P('aux', 'ao'), may hold values from -1 to 29, as said below
- coeff: bfloat16 [40960, 64], P('ao'), may hold values from -0.1875 to 0.1875
Outputs:
- relaid: bfloat16 [4096, 40960], P(('aux', 'ao'))
- pair_ints: float32 [4096, 64], P(('aux', 'ao'))
Inputs may be any that keep to these rules, and one draw needn't show every extreme that they name: `tile_col`: in the slots p * 768 // 64 .. of one device (aux index a, ao index p) the live ones come first and number between 5 and 12; in every draw some device has all 12 slots live. Empty slots hold -1. A live value c names AO column block 10 * (p - 1) + c, which lies inside the grid of 40960 functions.
All inputs are finite; a program needn't handle non-finite values.
Results may differ from a plain program's by a relative error of at most 0.007.
Values may be sent and summed in bfloat16 or wider, within the bound.
A program may use at most 64 MiB of HBM per device.

v0:
```python
import jax
import jax.numpy as jnp
from jax import lax
from jax.sharding import PartitionSpec as P

SCREEN_BLOCK = 64
OCC = 64
ORBITAL_BLOCKS = 10


def from_behind(shard, axis, by):
    size = lax.axis_size(axis)
    pairs = [(i, i + by) for i in range(size) if 0 <= i + by < size]
    return lax.ppermute(shard, axis, pairs)


def band_terms(tile_block, rows, columns, coeff_block):
    slots = rows.shape[0]
    blocks = coeff_block.reshape(ORBITAL_BLOCKS, SCREEN_BLOCK, OCC)
    picked = jnp.take(blocks, rows, axis=0)
    quads = tile_block.reshape(tile_block.shape[0], slots, SCREEN_BLOCK, SCREEN_BLOCK)
    half = jnp.einsum("tmi,qtmn->tqin", picked, quads, preferred_element_type=jnp.float32)
    placing = (columns[:, None] == jnp.arange(3 * ORBITAL_BLOCKS, dtype=jnp.int32)[None, :]).astype(
        jnp.float32
    )
    return jnp.einsum("tc,tqin->qicn", placing, half, precision=lax.Precision.HIGHEST)


def per_device(tiles, slot_row_block, tile_col, coeff):
    width = ORBITAL_BLOCKS * SCREEN_BLOCK
    band = band_terms(tiles, slot_row_block[0], tile_col[0], coeff)
    total_rows = band.shape[0] * band.shape[1]
    flattened = band.reshape(total_rows, 3 * width)
    from_before = from_behind(flattened[:, 2 * width :].astype(jnp.bfloat16), "ao", 1).astype(
        jnp.float32
    )
    source_following = from_behind(flattened[:, :width].astype(jnp.bfloat16), "ao", -1).astype(
        jnp.float32
    )
    owned = (flattened[:, width : 2 * width] + from_before + source_following).astype(jnp.bfloat16)
    relaid = lax.all_to_all(owned, "ao", split_axis=0, concat_axis=1, tiled=True)
    pair_ints = jnp.dot(
        relaid, lax.all_gather(coeff, "ao", axis=0, tiled=True), preferred_element_type=jnp.float32
    )
    return (relaid, pair_ints)


def solution(mesh):
    in_specs = (P("aux", "ao", None), P("aux", "ao"), P("aux", "ao"), P("ao", None))
    out_specs = (P(("aux", "ao"), None), P(("aux", "ao"), None))
    return jax.shard_map(
        per_device, mesh=mesh, in_specs=in_specs, out_specs=out_specs, check_vma=False
    )
```

profile of v0, /device:TPU:6, one launch (start us, length us, event | category | flops | bytes accessed | tf_op | source)
XLA Modules:
  0.0 137.3 jit_solution(10944115143796415142)
XLA Ops:
  7.2 0.0 all-gather.2.cloned.1.call-start
  7.2 0.7 all-gather.2.cloned.1.call-update
  7.9 1.0 copy.9
  8.9 2.5 %reshape.52 = bf16[8,12,64,64]{3,2,0,1:T(8,128)(2,1)S(1)} reshape(bf16[8,12,4096]{2,0,1:T(8,128)(2,1)} %param.4) | data formatting | bytes 1572864 | tf_op jit(solution)/shard_map/reshape | solution.py:21
  11.5 0.0 copy-start
  11.5 0.7 fusion.14
  12.2 0.6 gather_fusion
  12.8 0.7 compare_and_fusion
  13.4 0.7 convolution_bitcast_fusion
  14.1 0.0 copy-done
  14.1 7.7 %fusion.2 = f32[8,64,30,64]{3,2,1,0:T(8,128)} fusion(f32[12,8,64,64]{3,2,1,0:T(8,128)S(1)} %convolution_bitcast_fusion, s32[12]{0:T(128)S(1)} %bitcast.35), kind=kOutput, calls=%fused_computation.3 | convolution fusion | flops 141558112 | bytes 5505072 | tf_op jit(solution)/shard_map/tc,tqin->qicn/dot_general | solution.py:26
  21.8 7.7 %reshape.64 = f32[512,1920]{1,0:T(8,128)} reshape(f32[8,64,30,64]{3,2,1,0:T(8,128)} %fusion.2) | data formatting | bytes 7864320 | tf_op jit(solution)/shard_map/reshape | solution.py:33
  29.5 5.5 %copy.18 = f32[512,1920]{0,1:T(8,128)} copy(f32[512,1920]{1,0:T(8,128)} %reshape.64) | data formatting | bytes 7864320 | tf_op jit(solution)/shard_map/reshape | solution.py:33
  35.0 2.4 %convert.4 = bf16[512,1920]{0,1:T(8,128)(2,1)S(1)} convert(f32[512,1920]{0,1:T(8,128)} %copy.18) | non-fusion elementwise | flops 983040 | bytes 5898240 | tf_op jit(solution)/shard_map/convert.1
  37.3 0.1 fusion.16
  37.4 4.3 %collective-permute-start = (bf16[512,640]{0,1:T(8,128)(2,1)S(1)}, bf16[512,640]{0,1:T(8,128)(2,1)S(1)}, u32[]{:S(2)}, u32[]{:S(2)}) collective-permute-start(bf16[512,640]{0,1:T(8,128)(2,1)S(1)} %get-tuple-element.2), channel_id=1, source_target_pairs={{0,1},{1,2},{2,3},{3,4},{4,5},{5,6},{6,7},{7,8},{8,9},{9,10},{10,1... | collective-permute-start | bytes 1966088 | tf_op jit(solution)/shard_map/ppermute | solution.py:14
  41.8 1.3 collective-permute-start.1
  43.1 14.6 %collective-permute-done = bf16[512,640]{0,1:T(8,128)(2,1)S(1)} collective-permute-done((bf16[512,640]{0,1:T(8,128)(2,1)S(1)}, bf16[512,640]{0,1:T(8,128)(2,1)S(1)}, u32[]{:S(2)}, u32[]{:S(2)}) %collective-permute-start) | collective-permute-done | bytes 655392 | tf_op jit(solution)/shard_map/ppermute | solution.py:14
  57.7 4.3 %collective-permute-done.1 = bf16[512,640]{0,1:T(8,128)(2,1)S(1)} collective-permute-done((bf16[512,640]{0,1:T(8,128)(2,1)S(1)}, bf16[512,640]{0,1:T(8,128)(2,1)S(1)}, u32[]{:S(2)}, u32[]{:S(2)}) %collective-permute-start.1) | collective-permute-done | bytes 655392 | tf_op jit(solution)/shard_map/ppermute | solution.py:14
  62.0 1.7 %fusion.6 = bf16[512,640]{0,1:T(8,128)(2,1)S(1)} fusion(f32[512,1920]{0,1:T(8,128)} %copy.18, bf16[512,640]{0,1:T(8,128)(2,1)S(1)} %collective-permute-done.1, bf16[512,640]{0,1:T(8,128)(2,1)S(1)} %collective-permute-done), kind=kLoop, calls=%fused_computation.7 | loop fusion | flops 1638400 | bytes 3276800 | tf_op jit(solution)/shard_map/convert_element_type | solution.py:40
  63.6 0.3 copy.13
  63.9 40.9 %all_to_all.19 = bf16[64,8,640]{2,1,0:T(8,128)(2,1)S(1)} all-to-all(bf16[64,8,640]{2,1,0:T(8,128)(2,1)S(1)} %bitcast.33), channel_id=1, replica_groups=mesh['aux'=8,'ao'=64] {'ao'}, dimensions={0} | all-to-all | bytes 1310720 | tf_op jit(solution)/shard_map/all_to_all | solution.py:41
  104.8 20.3 %all-gather.2.cloned.1.call-done = bf16[40960,64]{0,1:T(8,128)(2,1)} async-done(((bf16[640,64]{0,1:T(8,128)(2,1)}), bf16[40960,64]{0,1:T(8,128)(2,1)}) %all-gather.2.cloned.1.call-update) | async-done | bytes 5242896 | tf_op jit(solution)/shard_map/all_gather | solution.py:43
  125.1 4.5 %fusion.17 = f32[8,64]{1,0:T(8,128)} fusion(bf16[8,40960]{1,0:T(8,128)(2,1)S(1)} %bitcast.31, bf16[40960,64]{0,1:T(8,128)(2,1)} %all-gather.2.cloned.1.call-done), kind=kOutput, calls=%fused_computation.22 | convolution fusion | flops 41943040 | bytes 5900288 | tf_op jit(solution)/shard_map/dot_general | solution.py:42
  129.6 0.8 copy.24
  (1 shorter events, 0.0 us)
Async XLA Ops:
  7.2 117.9 %all-gather.2.cloned.1.call-start = ((), (), s32[]{:S(2)}) async-start(), calls=%async_computation.1 | async-start | bytes 5324800 | tf_op jit(solution)/shard_map/all_gather | solution.py:43
  11.5 2.6 %copy-start = (s32[1,12]{1,0:T(1,128)S(1)}, s32[1,12]{1,0:T(1,128)}, u32[]{:S(2)}) copy-start(s32[1,12]{1,0:T(1,128)} %param.6) | copy-start | bytes 148
  37.4 20.2 %collective-permute-start = (bf16[512,640]{0,1:T(8,128)(2,1)S(1)}, bf16[512,640]{0,1:T(8,128)(2,1)S(1)}, u32[]{:S(2)}, u32[]{:S(2)}) collective-permute-start(bf16[512,640]{0,1:T(8,128)(2,1)S(1)} %get-tuple-element.2), channel_id=1, source_target_pairs={{0,1},{1,2},{2,3},{3,4},{4,5},{5,6},{6,7},{7,8},{8,9},{9,10},{10,1... | collective-permute-start | bytes 1966088 | tf_op jit(solution)/shard_map/ppermute | solution.py:14
  41.8 20.2 %collective-permute-start.1 = (bf16[512,640]{0,1:T(8,128)(2,1)S(1)}, bf16[512,640]{0,1:T(8,128)(2,1)S(1)}, u32[]{:S(2)}, u32[]{:S(2)}) collective-permute-start(bf16[512,640]{0,1:T(8,128)(2,1)S(1)} %get-tuple-element.3), channel_id=1, source_target_pairs={{1,0},{2,1},{3,2},{4,3},{5,4},{6,5},{7,6},{8,7},{9,8},{10,9},{11,1... | collective-permute-start | bytes 1966088 | tf_op jit(solution)/shard_map/ppermute | solution.py:14
Sparse Core Ops, SparseCore 0:
  11.1 113.9 all-gather.1
where the time goes:
time: 138 us; the launch traced here: 137 us
  blocking collectives  40.9 us (30%)
  waiting for transfers between devices  39.9 us (29%)
  local copies, waits for them, and re-layouts  18.6 us (13%)
  between operations  14.1 us (10%)
  matrix products  12.9 us (9%)
  starting transfers between devices  5.67 us (4%)
  other arithmetic  5.37 us (4%)
    all_to_all x1, blocking collectives, per_device(): lax.all_to_all(owned, 'ao', split_axis=0, concat_axis=1, tiled=True)  40.9 us
    all_gather x1, waiting for transfers between devices, per_device(): lax.all_gather(coeff, 'ao', axis=0, tiled=True)  20.3 us
    ppermute x2, waiting for transfers between devices, from_behind(): return lax.ppermute(shard, axis, pairs)  18.9 us
    reshape x2, local copies, waits for them, and re-layouts, per_device(): flattened = band.reshape(total_rows, 3 * width)  13.2 us
    dot_general x1, matrix products, band_terms(): jnp.einsum('tc,tqin->qicn', placing, half, precision=lax.Precision.HIGHEST)  7.66 us
    ppermute x2, starting transfers between devices, from_behind(): return lax.ppermute(shard, axis, pairs)  5.63 us
    dot_general x1, matrix products, per_device(): jnp.dot(relaid, lax.all_gather(coeff, 'ao', axis=0, tiled=True), preferre...  4.54 us
  transfers between devices with their start and end apart: 3, of which 3 were waited for; matrix products, arithmetic and copies ran while one was open for 23% of the time, Pallas kernels for 0%

commit v1 on v0

v1 whole, which is shorter than its diff:
```python
import jax
import jax.numpy as jnp
from jax import lax
from jax.experimental import pallas as pl
from jax.experimental.pallas import tpu as pltpu
from jax.sharding import PartitionSpec as P

SB = 64
OCC = 64
NB = 10
NT = 12
QD = 8
SIDE = 8
NAO = SIDE * SIDE
LANES = 128
GROUPS = 8
MESH = pl.DeviceIdType.MESH


def lower_half(shape):
    return lax.broadcasted_iota(jnp.int32, shape, len(shape) - 1) < SB


def swap_halves(x):
    return pltpu.roll(x, SB, axis=x.ndim - 1)


def doubled_blocks(coeff_ref, out_ref, first):
    for pair in range(NB // 2):
        x = coeff_ref[:, pair * LANES : (pair + 1) * LANES].astype(jnp.float32)
        y = swap_halves(x)
        low = lower_half(x.shape)
        out_ref[first + 2 * pair] = jnp.where(low, x, y).astype(jnp.bfloat16)
        out_ref[first + 2 * pair + 1] = jnp.where(low, y, x).astype(jnp.bfloat16)


def exchange_kernel(
    rows, cols, tiles, coeff, got, pair_got,
    raw, turned, send, halves, blocks, near, part, part_got, mid,
    load_sems, near_send, near_recv, main_send, main_recv, col_send, col_recv, row_send, row_recv, own_sems,
):
    aux, me = lax.axis_index("aux"), lax.axis_index("ao")
    y, z = me // SIDE, me % SIDE

    def partner(k):
        return ((y + k // SIDE) % SIDE) * SIDE + (z + k % SIDE) % SIDE

    barrier = pltpu.get_barrier_semaphore()

    @pl.loop(1, NAO)
    def _(k):
        pl.semaphore_signal(barrier, inc=1, device_id=(aux, partner(k)), device_id_type=MESH)

    loads = [pltpu.make_async_copy(tiles.at[pl.ds(4 * g, 4)], raw.at[pl.ds(4 * g, 4)], load_sems.at[g]) for g in range(3)]
    for load in loads:
        load.start()
    doubled_blocks(coeff, blocks, NB)

    for g in range(3):
        loads[g].wait()
        for sub in range(2):
            first = 4 * g + 2 * sub
            for side in range(2):
                for k in range(SB // 2):
                    v = raw[first + side, :, k * LANES : (k + 1) * LANES].astype(jnp.float32)
                    w = swap_halves(v)
                    turned[side, pl.ds(16 * k, 8), :] = v if side == 0 else w
                    turned[side, pl.ds(16 * k + 8, 8), :] = w if side == 0 else v
            left = []
            for side in range(2):
                t = first + side
                c = blocks[NB + rows[0, t]]
                left.append(jnp.where(cols[0, t] >= 0, c, jnp.zeros_like(c)))
            left = jnp.where(lower_half(left[0].shape), left[0], left[1])
            low = lower_half((SB, LANES))
            right = []
            for q in range(QD):
                a = turned[0, pl.ds(q, SB, stride=QD), :]
                b = turned[1, pl.ds(q, SB, stride=QD), :]
                right.append(jnp.concatenate([jnp.where(low, a, 0.0), jnp.where(low, 0.0, b)], axis=0).astype(jnp.bfloat16))
            half = jnp.dot(left, jnp.concatenate(right, axis=1), preferred_element_type=jnp.float32).astype(jnp.bfloat16)
            for q in range(QD):
                hq = half[:, q * LANES : (q + 1) * LANES]
                halves[2 * g + sub, pl.ds(q * OCC, OCC), :] = hq
                send[pl.ds(QD * q, QD), g, pl.ds(8 * sub, 8), :] = hq.reshape(SIDE, 8, LANES)

    pl.semaphore_wait(barrier, NAO - 1)

    near_copies = []
    for way, shift in ((0, 1), (1, NAO - 1)):
        near_copies.append(
            pltpu.make_async_remote_copy(
                coeff, near.at[way], near_send.at[way], near_recv.at[way],
                device_id=(aux, (me + shift) % NAO), device_id_type=MESH,
            )
        )
    for copy in near_copies:
        copy.start()

    own = pltpu.make_async_copy(send.at[me], got.at[me], own_sems.at[0])
    own.start()

    def ship(k):
        to = partner(k)
        pltpu.make_async_remote_copy(
            send.at[to], got.at[me], main_send, main_recv, device_id=(aux, to), device_id_type=MESH
        ).start()

    pl.loop(1, NAO // 4)(ship)

    for copy in near_copies:
        copy.wait()
    doubled_blocks(near.at[0], blocks, 0)
    doubled_blocks(near.at[1], blocks, 2 * NB)
    total = jnp.zeros((QD * OCC, LANES), jnp.float32)
    for s in range(NT // 2):
        w0 = blocks[jnp.maximum(cols[0, 2 * s], 0)]
        w1 = blocks[jnp.maximum(cols[0, 2 * s + 1], 0)]
        w = jnp.where(lower_half(w0.shape), w0, w1)
        total += lax.dot_general(
            halves[s], jnp.concatenate([w, w], axis=0), (((1,), (1,)), ((), ())), preferred_element_type=jnp.float32
        )
    high = total.astype(jnp.bfloat16)
    rest = (total - high.astype(jnp.float32)).astype(jnp.bfloat16)
    part[...] = jnp.where(lower_half(high.shape), high, rest).reshape(QD, OCC, LANES)

    own_part = pltpu.make_async_copy(part.at[y], part_got.at[y], own_sems.at[1])
    own_part.start()

    @pl.loop(1, SIDE)
    def _(k):
        to = (y + k) % SIDE
        pltpu.make_async_remote_copy(
            part.at[to], part_got.at[y], col_send, col_recv, device_id=(aux, to * SIDE + z), device_id_type=MESH
        ).start()

    pl.loop(NAO // 4, NAO)(ship)

    seven = pl.ds(0, SIDE - 1)
    own_part.wait()
    pltpu.make_async_copy(part_got.at[seven], part_got.at[seven], col_recv).wait()
    summed = part_got[0].astype(jnp.float32)
    for k in range(1, SIDE):
        summed += part_got[k].astype(jnp.float32)
    summed += swap_halves(summed)
    mid[...] = summed.reshape(SIDE, 8, LANES)
    own_mid = pltpu.make_async_copy(mid.at[z], pair_got.at[z], own_sems.at[2])
    own_mid.start()

    @pl.loop(1, SIDE)
    def _(k):
        to = (z + k) % SIDE
        pltpu.make_async_remote_copy(
            mid.at[to], pair_got.at[z], row_send, row_recv, device_id=(aux, y * SIDE + to), device_id_type=MESH
        ).start()

    own.wait()
    own_mid.wait()
    most = pl.ds(0, NAO - 1)
    pltpu.make_async_copy(part.at[seven], part.at[seven], col_send).wait()
    pltpu.make_async_copy(mid.at[seven], mid.at[seven], row_send).wait()
    pltpu.make_async_copy(send.at[most], send.at[most], main_send).wait()
    pltpu.make_async_copy(pair_got.at[seven], pair_got.at[seven], row_recv).wait()
    pltpu.make_async_copy(got.at[most], got.at[most], main_recv).wait()


def exchange(rows, cols, tiles, coeff):
    vmem, smem = pl.BlockSpec(memory_space=pltpu.VMEM), pl.BlockSpec(memory_space=pltpu.SMEM)
    dma = pltpu.SemaphoreType.DMA
    bf16, f32 = jnp.bfloat16, jnp.float32
    return pl.pallas_call(
        exchange_kernel,
        out_shape=(
            jax.ShapeDtypeStruct((NAO, 3, 16, LANES), bf16),
            jax.ShapeDtypeStruct((SIDE, 8, LANES), f32),
        ),
        in_specs=[smem, smem, pl.BlockSpec(memory_space=pl.ANY), vmem],
        out_specs=(vmem, vmem),
        scratch_shapes=[
            pltpu.VMEM((NT, QD, SB * SB), bf16),
            pltpu.VMEM((2, SB * QD, LANES), f32),
            pltpu.VMEM((NAO, 3, 16, LANES), bf16),
            pltpu.VMEM((NT // 2, QD * OCC, LANES), bf16),
            pltpu.VMEM((3 * NB, OCC, LANES), bf16),
            pltpu.VMEM((2, OCC, NB * SB), bf16),
            pltpu.VMEM((QD, OCC, LANES), bf16),
            pltpu.VMEM((SIDE, OCC, LANES), bf16),
            pltpu.VMEM((SIDE, 8, LANES), f32),
            dma((3,)), dma((2,)), dma((2,)), dma, dma, dma, dma, dma, dma, dma((3,)),
        ],
        compiler_params=pltpu.CompilerParams(collective_id=0, has_side_effects=True, vmem_limit_bytes=40 << 20),
        cost_estimate=pl.CostEstimate(flops=200_000_000, bytes_accessed=3_000_000, transcendentals=0),
        name="half_transform_exchange",
    )(rows, cols, tiles, coeff)


def place_kernel(cols, got, pair_got, relaid, pair_ints, *sums):
    per = NAO // GROUPS
    tiles_per = NB // 2
    zero = jnp.zeros((8, LANES), jnp.float32)
    for total in sums:
        total[...] = jnp.zeros(total.shape, jnp.float32)
    half_of = lax.broadcasted_iota(jnp.int32, (8, LANES), 1) // SB
    low = half_of == 0

    @pl.loop(0, per)
    def _(k):
        for s in range(NT // 2):
            for g in range(GROUPS):
                p = g * per + k
                v = got[p, s // 2, pl.ds(8 * (s % 2), 8), :].astype(jnp.float32)
                w = swap_halves(v)
                for side in range(2):
                    both = jnp.where(low, v, w) if side == 0 else jnp.where(low, w, v)
                    c = jnp.maximum(cols[0, p * NT + 2 * s + side], 0)
                    at = tiles_per * k + c // 2
                    sums[g][at] += jnp.where(half_of == c % 2, both, zero)

    for tile in range(NAO * tiles_per):
        g, local = divmod(tile, per * tiles_per)
        value = sums[g][local + tiles_per]
        if local < tiles_per and g > 0:
            value += sums[g - 1][local + (per + 1) * tiles_per]
        if local >= (per - 1) * tiles_per and g < GROUPS - 1:
            value += sums[g + 1][local - (per - 1) * tiles_per]
        relaid[:, tile * LANES : (tile + 1) * LANES] = value.astype(jnp.bfloat16)

    total = pair_got[0]
    for k in range(1, SIDE):
        total += pair_got[k]
    pair_ints[...] = total[:, :OCC]


def place(cols, got, pair_got):
    vmem, smem = pl.BlockSpec(memory_space=pltpu.VMEM), pl.BlockSpec(memory_space=pltpu.SMEM)
    per = NAO // GROUPS
    return pl.pallas_call(
        place_kernel,
        out_shape=(
            jax.ShapeDtypeStruct((8, NAO * NB * SB), jnp.bfloat16),
            jax.ShapeDtypeStruct((8, OCC), jnp.float32),
        ),
        in_specs=[smem, vmem, vmem],
        out_specs=(vmem, vmem),
        scratch_shapes=[pltpu.VMEM(((per + 2) * NB // 2, 8, LANES), jnp.float32)] * GROUPS,
        compiler_params=pltpu.CompilerParams(vmem_limit_bytes=40 << 20),
        cost_estimate=pl.CostEstimate(flops=1_000_000, bytes_accessed=1_500_000, transcendentals=0),
        name="place",
    )(cols, got, pair_got)


def per_device(tiles, slot_row_block, tile_col, coeff):
    all_cols = lax.all_gather(tile_col, "ao", axis=1, tiled=True)
    got, pair_got = exchange(slot_row_block, tile_col, jnp.transpose(tiles, (1, 0, 2)), coeff.T)
    return place(all_cols, got, pair_got)


def solution(mesh):
    in_specs = (P("aux", "ao", None), P("aux", "ao"), P("aux", "ao"), P("ao", None))
    out_specs = (P(("aux", "ao"), None), P(("aux", "ao"), None))
    return jax.shard_map(per_device, mesh=mesh, in_specs=in_specs, out_specs=out_specs, check_vma=False)
```

time: 138 us -> 73.2 us (0.53)
  waiting for transfers between devices: 39.9 us -> 0 us
  Pallas kernels: 0 us -> 36 us
  local copies, waits for them, and re-layouts: 18.6 us -> 4.67 us
  matrix products: 12.9 us -> 0 us
  between operations: 14.1 us -> 1.31 us
  blocking collectives: 40.9 us -> 30.9 us
  starting transfers between devices: 5.67 us -> 0 us
  other arithmetic: 5.37 us -> 0 us
    all_to_all x1 -> x0, blocking collectives: 40.9 us -> none  [per_device(): lax.all_to_all(owned, 'ao', split_axis=0, concat_axis=1, tiled=True)]
    pallas_call x0 -> x2, Pallas kernels: none -> 36 us  [the longest x1 31.1 us: exchange(): pl.pallas_call(exchange_kernel, out_shape=(jax.ShapeDtypeStruct((NAO, 3,...]
    unnamed x0 -> x1, blocking collectives: none -> 30.9 us
    all_gather x1 -> x0, waiting for transfers between devices: 20.3 us -> none  [per_device(): lax.all_gather(coeff, 'ao', axis=0, tiled=True)]
    ppermute x2 -> x0, waiting for transfers between devices: 18.9 us -> none  [from_behind(): return lax.ppermute(shard, axis, pairs)]
    reshape x3 -> x0, local copies, waits for them, and re-layouts: 15.7 us -> none  [the longest x2 13.2 us: per_device(): flattened = band.reshape(total_rows, 3 * width)]
    dot_general x3 -> x0, matrix products: 12.9 us -> none  [the longest x1 7.66 us: band_terms(): jnp.einsum('tc,tqin->qicn', placing, half, precision=lax.Precision.HIGHEST)]
    ppermute x2 -> x0, starting transfers between devices: 5.63 us -> none  [from_behind(): return lax.ppermute(shard, axis, pairs)]
  transfers between devices with their start and end apart: 3 -> 0, of which waited for: 3 -> 0; matrix products, arithmetic and copies ran while one was open for 23% -> 0% of each run, Pallas kernels for 0% -> 0%
where the time goes in v1:
time: 73.2 us; the launch traced here: 72.9 us
  Pallas kernels  36 us (49%)
  blocking collectives  30.9 us (42%)
  local copies, waits for them, and re-layouts  4.67 us (6%)
  between operations  1.31 us (2%)
    pallas_call x1, Pallas kernels, exchange(): pl.pallas_call(exchange_kernel, out_shape=(jax.ShapeDtypeStruct((NAO, 3,...  31.1 us
    unnamed x1, blocking collectives  30.9 us
    pallas_call x1, Pallas kernels, place(): pl.pallas_call(place_kernel, out_shape=(jax.ShapeDtypeStruct((8, NAO * NB...  4.86 us
    unnamed x12, local copies, waits for them, and re-layouts  4.67 us

profile of v1, /device:TPU:6, one launch (start us, length us, event | category | flops | bytes accessed | tf_op | source)
XLA Modules:
  0.0 72.9 jit_solution(16897730215190396901)
XLA Ops:
  0.6 1.3 %dynamic-slice = u32[1]{0:T(128)} dynamic-slice(u32[512]{0:T(512)} %constant.5, u32[]{:T(128)S(6)} %add), dynamic_slice_sizes={1} | dynamic-slice | bytes 12
  2.6 0.0 copy-start.2
  2.6 0.6 copy-done.2
  3.2 0.1 bitcast_dynamic-update-slice_fusion
  3.3 30.9 %all-reduce = s32[768]{0:T(1024)S(1)} all-reduce(s32[768]{0:T(1024)S(1)} %bitcast_dynamic-update-slice_fusion), channel_id=1, replica_groups=mesh['aux'=8,'ao'=64] {'ao'}, use_global_device_ids=true, to_apply=%add | all-reduce | flops 768 | bytes 6144
  34.2 0.0 copy-start.3
  34.2 0.6 copy-done.3
  34.9 0.0 copy-start
  34.9 1.1 %copy-done = bf16[8,12,4096]{2,0,1:T(8,128)(2,1)S(1)} copy-done((bf16[8,12,4096]{2,0,1:T(8,128)(2,1)S(1)}, bf16[8,12,4096]{2,0,1:T(8,128)(2,1)}, u32[]{:S(2)}) %copy-start) | copy-done | bytes 786456
  36.0 0.0 copy-start.1
  36.0 0.9 %copy-done.1 = bf16[640,64]{0,1:T(8,128)(2,1)S(1)} copy-done((bf16[640,64]{0,1:T(8,128)(2,1)S(1)}, bf16[640,64]{0,1:T(8,128)(2,1)}, u32[]{:S(2)}) %copy-start.1) | copy-done | bytes 81944
  36.9 31.1 %half_transform_exchange.1 = (bf16[64,3,16,128]{3,2,1,0:T(8,128)(2,1)S(1)}, f32[8,8,128]{2,1,0:T(8,128)S(1)}) custom-call(s32[1,12]{1,0:T(1,128)S(1)} %copy-done.3, s32[1,12]{1,0:T(1,128)S(1)} %copy-done.2, bf16[12,8,4096]{2,1,0:T(8,128)(2,1)S(1)} %bitcast.5, bf16[64,640]{1,0:T(8,128)(2,1)S(1)} %bitcast.6), custom_call_target="tpu_custom_call" | custom-call | flops 200000000 | bytes 3000000 | tf_op jit(solution)/shard_map/half_transform_exchange/pallas_call | solution.py:171
  68.0 4.9 %place.1 = (bf16[8,40960]{1,0:T(8,128)(2,1)}, f32[8,64]{1,0:T(8,128)}) custom-call(s32[1,768]{1,0:T(1,128)S(1)} %reshape.6.cols, bf16[64,3,16,128]{3,2,1,0:T(8,128)(2,1)S(1)} %get-tuple-element.4.got, f32[8,8,128]{2,1,0:T(8,128)S(1)} %get-tuple-element.5.pair_got), custom_call_target="tpu_custom_call" | custom-call | flops 1000000 | bytes 1500000 | tf_op jit(solution)/shard_map/place/pallas_call | solution.py:237
  (2 shorter events, 0.0 us)
Async XLA Ops:
  2.6 0.7 copy-start.2
  34.2 0.7 copy-start.3
  34.9 1.1 %copy-start = (bf16[8,12,4096]{2,0,1:T(8,128)(2,1)S(1)}, bf16[8,12,4096]{2,0,1:T(8,128)(2,1)}, u32[]{:S(2)}) copy-start(bf16[8,12,4096]{2,0,1:T(8,128)(2,1)} %param.4) | copy-start | bytes 2359300
  36.0 0.9 %copy-start.1 = (bf16[640,64]{0,1:T(8,128)(2,1)S(1)}, bf16[640,64]{0,1:T(8,128)(2,1)}, u32[]{:S(2)}) copy-start(bf16[640,64]{0,1:T(8,128)(2,1)} %param.7) | copy-start | bytes 245764

commit v2 on v1

--- a/solution.py
+++ b/solution.py
@@ -13,7 +13,7 @@
 SIDE = 8
 NAO = SIDE * SIDE
 LANES = 128
-GROUPS = 8
+GROUPS = SIDE
 MESH = pl.DeviceIdType.MESH
 
 
@@ -35,25 +35,43 @@
 
 
 def exchange_kernel(
-    rows, cols, tiles, coeff, got, pair_got,
-    raw, turned, send, halves, blocks, near, part, part_got, mid,
-    load_sems, near_send, near_recv, main_send, main_recv, col_send, col_recv, row_send, row_recv, own_sems,
+    rows_hbm, cols_hbm, tiles, coeff_hbm, got, pair_got,
+    rows, cols, coeff, raw, turned, send, halves, blocks, near, part, part_got, mid,
+    ready, small_sems, load_sems, near_send, near_recv, main_send, main_recv, col_send, col_recv, row_send, row_recv, own_sems,
 ):
     aux, me = lax.axis_index("aux"), lax.axis_index("ao")
     y, z = me // SIDE, me % SIDE
 
-    def partner(k):
-        return ((y + k // SIDE) % SIDE) * SIDE + (z + k % SIDE) % SIDE
-
     barrier = pltpu.get_barrier_semaphore()
 
-    @pl.loop(1, NAO)
-    def _(k):
-        pl.semaphore_signal(barrier, inc=1, device_id=(aux, partner(k)), device_id_type=MESH)
-
+    smalls = [
+        pltpu.make_async_copy(a, b, small_sems.at[i])
+        for i, (a, b) in enumerate(((coeff_hbm, coeff), (rows_hbm, rows), (cols_hbm, cols)))
+    ]
+    for small in smalls:
+        small.start()
     loads = [pltpu.make_async_copy(tiles.at[pl.ds(4 * g, 4)], raw.at[pl.ds(4 * g, 4)], load_sems.at[g]) for g in range(3)]
     for load in loads:
         load.start()
+
+    @pl.loop(1, SIDE)
+    def _(k):
+        pl.semaphore_signal(barrier, inc=1, device_id=(aux, y * SIDE + (z + k) % SIDE), device_id_type=MESH)
+        pl.semaphore_signal(barrier, inc=1, device_id=(aux, (y + k) % SIDE * SIDE + z), device_id_type=MESH)
+
+    for shift in (1, NAO - 1):
+        pl.semaphore_signal(barrier, inc=1, device_id=(aux, (me + shift) % NAO), device_id_type=MESH)
+
+    near_copies = [
+        pltpu.make_async_remote_copy(
+            coeff, near.at[way], near_send.at[way], near_recv.at[way],
+            device_id=(aux, (me + shift) % NAO), device_id_type=MESH,
+        )
+        for way, shift in ((0, 1), (1, NAO - 1))
+    ]
+
+    for small in smalls:
+        small.wait()
     doubled_blocks(coeff, blocks, NB)
 
     for g in range(3):
@@ -83,30 +101,30 @@
                 hq = half[:, q * LANES : (q + 1) * LANES]
                 halves[2 * g + sub, pl.ds(q * OCC, OCC), :] = hq
                 send[pl.ds(QD * q, QD), g, pl.ds(8 * sub, 8), :] = hq.reshape(SIDE, 8, LANES)
-
-    pl.semaphore_wait(barrier, NAO - 1)
-
-    near_copies = []
-    for way, shift in ((0, 1), (1, NAO - 1)):
-        near_copies.append(
-            pltpu.make_async_remote_copy(
-                coeff, near.at[way], near_send.at[way], near_recv.at[way],
-                device_id=(aux, (me + shift) % NAO), device_id_type=MESH,
-            )
-        )
-    for copy in near_copies:
-        copy.start()
+        if g == 0:
+            pl.semaphore_wait(barrier, 2 * SIDE)
+            for copy in near_copies:
+                copy.start()
+
+            @pl.loop(1, SIDE)
+            def _(k):
+                pl.semaphore_signal(
+                    ready.at[SIDE - k], inc=1, device_id=(aux, y * SIDE + (z + k) % SIDE), device_id_type=MESH
+                )
 
     own = pltpu.make_async_copy(send.at[me], got.at[me], own_sems.at[0])
     own.start()
 
-    def ship(k):
-        to = partner(k)
+    def ship(dy, dz):
+        to = (y + dy) % SIDE * SIDE + (z + dz) % SIDE
         pltpu.make_async_remote_copy(
             send.at[to], got.at[me], main_send, main_recv, device_id=(aux, to), device_id_type=MESH
         ).start()
 
-    pl.loop(1, NAO // 4)(ship)
+    @pl.loop(1, SIDE)
+    def _(k):
+        ship(k, 0)
+        ship(0, k)
 
     for copy in near_copies:
         copy.wait()
@@ -122,7 +140,13 @@
         )
     high = total.astype(jnp.bfloat16)
     rest = (total - high.astype(jnp.float32)).astype(jnp.bfloat16)
-    part[...] = jnp.where(lower_half(high.shape), high, rest).reshape(QD, OCC, LANES)
+    part[:, pl.ds(0, OCC), :] = jnp.where(lower_half(high.shape), high, rest).reshape(QD, OCC, LANES)
+    lane = lax.broadcasted_iota(jnp.int32, (16, LANES), 1)
+    columns = jnp.zeros((16, LANES), jnp.float32)
+    for t in range(NT):
+        columns = jnp.where(lane == 16 * z + t, jnp.maximum(cols[0, t], 0).astype(jnp.float32), columns)
+    for q in range(QD):
+        part[q, pl.ds(OCC, 16), :] = columns.astype(jnp.bfloat16)
 
     own_part = pltpu.make_async_copy(part.at[y], part_got.at[y], own_sems.at[1])
     own_part.start()
@@ -134,16 +158,28 @@
             part.at[to], part_got.at[y], col_send, col_recv, device_id=(aux, to * SIDE + z), device_id_type=MESH
         ).start()
 
-    pl.loop(NAO // 4, NAO)(ship)
+    @pl.loop(1, SIDE)
+    def _(k):
+        pl.semaphore_wait(ready.at[k], 1)
+
+        @pl.loop(1, SIDE)
+        def _(j):
+            ship(j, k)
 
     seven = pl.ds(0, SIDE - 1)
     own_part.wait()
     pltpu.make_async_copy(part_got.at[seven], part_got.at[seven], col_recv).wait()
-    summed = part_got[0].astype(jnp.float32)
+    arrived = part_got[0].astype(jnp.float32)
+    summed, columns = arrived[:OCC], arrived[OCC : OCC + 8]
+    row = lax.broadcasted_iota(jnp.int32, columns.shape, 0)
     for k in range(1, SIDE):
-        summed += part_got[k].astype(jnp.float32)
+        arrived = part_got[k].astype(jnp.float32)
+        summed += arrived[:OCC]
+        columns = jnp.where(row == k, arrived[OCC : OCC + 8], columns)
     summed += swap_halves(summed)
-    mid[...] = summed.reshape(SIDE, 8, LANES)
+    mid[:, pl.ds(0, 8), :] = summed.reshape(SIDE, 8, LANES)
+    for k in range(SIDE):
+        mid[k, pl.ds(8, 8), :] = columns
     own_mid = pltpu.make_async_copy(mid.at[z], pair_got.at[z], own_sems.at[2])
     own_mid.start()
 
@@ -165,28 +201,31 @@
 
 
 def exchange(rows, cols, tiles, coeff):
-    vmem, smem = pl.BlockSpec(memory_space=pltpu.VMEM), pl.BlockSpec(memory_space=pltpu.SMEM)
+    vmem, hbm = pl.BlockSpec(memory_space=pltpu.VMEM), pl.BlockSpec(memory_space=pltpu.HBM)
     dma = pltpu.SemaphoreType.DMA
     bf16, f32 = jnp.bfloat16, jnp.float32
     return pl.pallas_call(
         exchange_kernel,
         out_shape=(
             jax.ShapeDtypeStruct((NAO, 3, 16, LANES), bf16),
-            jax.ShapeDtypeStruct((SIDE, 8, LANES), f32),
+            jax.ShapeDtypeStruct((SIDE, 16, LANES), f32),
         ),
-        in_specs=[smem, smem, pl.BlockSpec(memory_space=pl.ANY), vmem],
+        in_specs=[hbm, hbm, hbm, hbm],
         out_specs=(vmem, vmem),
         scratch_shapes=[
+            pltpu.SMEM((1, NT), jnp.int32),
+            pltpu.SMEM((1, NT), jnp.int32),
+            pltpu.VMEM((OCC, NB * SB), bf16),
             pltpu.VMEM((NT, QD, SB * SB), bf16),
             pltpu.VMEM((2, SB * QD, LANES), f32),
             pltpu.VMEM((NAO, 3, 16, LANES), bf16),
             pltpu.VMEM((NT // 2, QD * OCC, LANES), bf16),
             pltpu.VMEM((3 * NB, OCC, LANES), bf16),
             pltpu.VMEM((2, OCC, NB * SB), bf16),
-            pltpu.VMEM((QD, OCC, LANES), bf16),
-            pltpu.VMEM((SIDE, OCC, LANES), bf16),
-            pltpu.VMEM((SIDE, 8, LANES), f32),
-            dma((3,)), dma((2,)), dma((2,)), dma, dma, dma, dma, dma, dma, dma((3,)),
+            pltpu.VMEM((QD, OCC + 16, LANES), bf16),
+            pltpu.VMEM((SIDE, OCC + 16, LANES), bf16),
+            pltpu.VMEM((SIDE, 16, LANES), f32),
+            pltpu.SemaphoreType.REGULAR((SIDE,)), dma((3,)), dma((3,)), dma((2,)), dma((2,)), dma, dma, dma, dma, dma, dma, dma((3,)),
         ],
         compiler_params=pltpu.CompilerParams(collective_id=0, has_side_effects=True, vmem_limit_bytes=40 << 20),
         cost_estimate=pl.CostEstimate(flops=200_000_000, bytes_accessed=3_000_000, transcendentals=0),
@@ -194,14 +233,21 @@
     )(rows, cols, tiles, coeff)
 
 
-def place_kernel(cols, got, pair_got, relaid, pair_ints, *sums):
+def place_kernel(got, pair_got, relaid, pair_ints, cols_vmem, cols, cols_sem, *sums):
     per = NAO // GROUPS
     tiles_per = NB // 2
     zero = jnp.zeros((8, LANES), jnp.float32)
+    columns = pair_got[0, pl.ds(8, 8), :]
+    for k in range(1, SIDE):
+        columns += pair_got[k, pl.ds(8, 8), :]
+    cols_vmem[...] = columns.astype(jnp.int32)
+    fetch = pltpu.make_async_copy(cols_vmem, cols, cols_sem)
+    fetch.start()
     for total in sums:
         total[...] = jnp.zeros(total.shape, jnp.float32)
     half_of = lax.broadcasted_iota(jnp.int32, (8, LANES), 1) // SB
     low = half_of == 0
+    fetch.wait()
 
     @pl.loop(0, per)
     def _(k):
@@ -212,9 +258,9 @@
                 w = swap_halves(v)
                 for side in range(2):
                     both = jnp.where(low, v, w) if side == 0 else jnp.where(low, w, v)
-                    c = jnp.maximum(cols[0, p * NT + 2 * s + side], 0)
-                    at = tiles_per * k + c // 2
-                    sums[g][at] += jnp.where(half_of == c % 2, both, zero)
+                    c = cols[g, 16 * k + 2 * s + side]
+                    at = tiles_per * k + lax.shift_right_logical(c, 1)
+                    sums[g][at] += jnp.where(half_of == jnp.bitwise_and(c, 1), both, zero)
 
     for tile in range(NAO * tiles_per):
         g, local = divmod(tile, per * tiles_per)
@@ -225,14 +271,14 @@
             value += sums[g + 1][local - (per - 1) * tiles_per]
         relaid[:, tile * LANES : (tile + 1) * LANES] = value.astype(jnp.bfloat16)
 
-    total = pair_got[0]
+    total = pair_got[0, pl.ds(0, 8), :]
     for k in range(1, SIDE):
-        total += pair_got[k]
+        total += pair_got[k, pl.ds(0, 8), :]
     pair_ints[...] = total[:, :OCC]
 
 
-def place(cols, got, pair_got):
-    vmem, smem = pl.BlockSpec(memory_space=pltpu.VMEM), pl.BlockSpec(memory_space=pltpu.SMEM)
+def place(got, pair_got):
+    vmem = pl.BlockSpec(memory_space=pltpu.VMEM)
     per = NAO // GROUPS
     return pl.pallas_call(
         place_kernel,
@@ -240,19 +286,24 @@
             jax.ShapeDtypeStruct((8, NAO * NB * SB), jnp.bfloat16),
             jax.ShapeDtypeStruct((8, OCC), jnp.float32),
         ),
-        in_specs=[smem, vmem, vmem],
+        in_specs=[vmem, vmem],
         out_specs=(vmem, vmem),
-        scratch_shapes=[pltpu.VMEM(((per + 2) * NB // 2, 8, LANES), jnp.float32)] * GROUPS,
+        scratch_shapes=[
+            pltpu.VMEM((SIDE, LANES), jnp.int32),
+            pltpu.SMEM((SIDE, LANES), jnp.int32),
+            pltpu.SemaphoreType.DMA,
+            *[pltpu.VMEM(((per + 2) * NB // 2, 8, LANES), jnp.float32)] * GROUPS,
+        ],
         compiler_params=pltpu.CompilerParams(vmem_limit_bytes=40 << 20),
         cost_estimate=pl.CostEstimate(flops=1_000_000, bytes_accessed=1_500_000, transcendentals=0),
         name="place",
-    )(cols, got, pair_got)
+    )(got, pair_got)
 
 
 def per_device(tiles, slot_row_block, tile_col, coeff):
-    all_cols = lax.all_gather(tile_col, "ao", axis=1, tiled=True)
-    got, pair_got = exchange(slot_row_block, tile_col, jnp.transpose(tiles, (1, 0, 2)), coeff.T)
-    return place(all_cols, got, pair_got)
+    operands = slot_row_block, tile_col, jnp.transpose(tiles, (1, 0, 2)), coeff.T
+    got, pair_got = exchange(*(pltpu.with_memory_space_constraint(x, pltpu.HBM) for x in operands))
+    return place(got, pair_got)
 
 
 def solution(mesh):

time: 73.2 us -> 49.7 us (0.68)
  blocking collectives: 30.9 us -> 0 us
  Pallas kernels: 36 us -> 48.8 us
  local copies, waits for them, and re-layouts: 4.67 us -> 0 us
    unnamed x1 -> x0, blocking collectives: 30.9 us -> none
    pallas_call x1, Pallas kernels: 31.1 us -> 45 us  [exchange(): pl.pallas_call(exchange_kernel, out_shape=(jax.ShapeDtypeStruct((NAO, 3,...]
    unnamed x12 -> x0, local copies, waits for them, and re-layouts: 4.67 us -> none
    pallas_call x1, Pallas kernels: 4.86 us -> 3.73 us  [place(): pl.pallas_call(place_kernel, out_shape=(jax.ShapeDtypeStruct((8, NAO * NB...]
where the time goes in v2:
time: 49.7 us; the launch traced here: 49.4 us
  Pallas kernels  48.8 us (98%)
  between operations  0.64 us (1%)
    pallas_call x1, Pallas kernels, exchange(): pl.pallas_call(exchange_kernel, out_shape=(jax.ShapeDtypeStruct((NAO, 3,...  45 us
    pallas_call x1, Pallas kernels, place(): pl.pallas_call(place_kernel, out_shape=(jax.ShapeDtypeStruct((8, NAO * NB...  3.73 us

profile of v2, /device:TPU:6, one launch (start us, length us, event | category | flops | bytes accessed | tf_op | source)
XLA Modules:
  0.0 49.4 jit_solution(14804469676759618736)
XLA Ops:
  0.6 45.0 %half_transform_exchange.1 = (bf16[64,3,16,128]{3,2,1,0:T(8,128)(2,1)S(1)}, f32[8,16,128]{2,1,0:T(8,128)S(1)}) custom-call(s32[1,12]{1,0:T(1,128)} %rows_hbm.1, s32[1,12]{1,0:T(1,128)} %cols_hbm.1, bf16[12,8,4096]{2,1,0:T(8,128)(2,1)} %bitcast.2, bf16[64,640]{1,0:T(8,128)(2,1)} %bitcast.3), custom_call_target="tpu_custom_call" | custom-call | flops 200000000 | bytes 3000000 | tf_op jit(solution)/shard_map/half_transform_exchange/pallas_call | solution.py:207
  45.7 3.7 %place.1 = (bf16[8,40960]{1,0:T(8,128)(2,1)}, f32[8,64]{1,0:T(8,128)}) custom-call(bf16[64,3,16,128]{3,2,1,0:T(8,128)(2,1)S(1)} %get-tuple-element.4.got, f32[8,16,128]{2,1,0:T(8,128)S(1)} %get-tuple-element.5.pair_got), custom_call_target="tpu_custom_call" | custom-call | flops 1000000 | bytes 1500000 | tf_op jit(solution)/shard_map/place/pallas_call | solution.py:283

commit v3 on v2

--- a/solution.py
+++ b/solution.py
@@ -15,6 +15,7 @@
 LANES = 128
 GROUPS = SIDE
 MESH = pl.DeviceIdType.MESH
+FAR_FIRST = (4, 3, -3, 2, -2, 1, -1)
 
 
 def lower_half(shape):
@@ -116,15 +117,21 @@
     own.start()
 
     def ship(dy, dz):
-        to = (y + dy) % SIDE * SIDE + (z + dz) % SIDE
+        to = (y + dy + SIDE) % SIDE * SIDE + (z + dz + SIDE) % SIDE
         pltpu.make_async_remote_copy(
             send.at[to], got.at[me], main_send, main_recv, device_id=(aux, to), device_id_type=MESH
         ).start()
 
-    @pl.loop(1, SIDE)
-    def _(k):
-        ship(k, 0)
-        ship(0, k)
+    for far in FAR_FIRST:
+        ship(far, 0)
+        ship(0, far)
+
+    def ship_column(k):
+        pl.semaphore_wait(ready.at[k % SIDE], 1)
+        for j in FAR_FIRST:
+            ship(j, k)
+
+    ship_column(FAR_FIRST[0])
 
     for copy in near_copies:
         copy.wait()
@@ -158,13 +165,8 @@
             part.at[to], part_got.at[y], col_send, col_recv, device_id=(aux, to * SIDE + z), device_id_type=MESH
         ).start()
 
-    @pl.loop(1, SIDE)
-    def _(k):
-        pl.semaphore_wait(ready.at[k], 1)
-
-        @pl.loop(1, SIDE)
-        def _(j):
-            ship(j, k)
+    for k in FAR_FIRST[1:]:
+        ship_column(k)
 
     seven = pl.ds(0, SIDE - 1)
     own_part.wait()

time: 49.7 us -> 43.3 us (0.87)
  Pallas kernels: 48.8 us -> 42.6 us
    pallas_call x1, Pallas kernels: 45 us -> 38.8 us  [exchange(): pl.pallas_call(exchange_kernel, out_shape=(jax.ShapeDtypeStruct((NAO, 3,...]
where the time goes in v3:
time: 43.3 us; the launch traced here: 43.2 us
  Pallas kernels  42.6 us (98%)
  between operations  0.64 us (1%)
    pallas_call x1, Pallas kernels, exchange(): pl.pallas_call(exchange_kernel, out_shape=(jax.ShapeDtypeStruct((NAO, 3,...  38.8 us
    pallas_call x1, Pallas kernels, place(): pl.pallas_call(place_kernel, out_shape=(jax.ShapeDtypeStruct((8, NAO * NB...  3.74 us

profile of v3, /device:TPU:6, one launch (start us, length us, event | category | flops | bytes accessed | tf_op | source)
XLA Modules:
  0.0 43.2 jit_solution(15371758138955375365)
XLA Ops:
  0.6 38.8 %half_transform_exchange.1 = (bf16[64,3,16,128]{3,2,1,0:T(8,128)(2,1)S(1)}, f32[8,16,128]{2,1,0:T(8,128)S(1)}) custom-call(s32[1,12]{1,0:T(1,128)} %rows_hbm.1, s32[1,12]{1,0:T(1,128)} %cols_hbm.1, bf16[12,8,4096]{2,1,0:T(8,128)(2,1)} %bitcast.2, bf16[64,640]{1,0:T(8,128)(2,1)} %bitcast.3), custom_call_target="tpu_custom_call" | custom-call | flops 200000000 | bytes 3000000 | tf_op jit(solution)/shard_map/half_transform_exchange/pallas_call | solution.py:209
  39.5 3.7 %place.1 = (bf16[8,40960]{1,0:T(8,128)(2,1)}, f32[8,64]{1,0:T(8,128)}) custom-call(bf16[64,3,16,128]{3,2,1,0:T(8,128)(2,1)S(1)} %get-tuple-element.4.got, f32[8,16,128]{2,1,0:T(8,128)S(1)} %get-tuple-element.5.pair_got), custom_call_target="tpu_custom_call" | custom-call | flops 1000000 | bytes 1500000 | tf_op jit(solution)/shard_map/place/pallas_call | solution.py:285

commit v4 on v2

--- a/solution.py
+++ b/solution.py
@@ -15,6 +15,19 @@
 LANES = 128
 GROUPS = SIDE
 MESH = pl.DeviceIdType.MESH
+REACH = SIDE
+
+
+def offsets_at(hops):
+    near = range(1 - SIDE // 2, SIDE // 2 + 1)
+    found = []
+    for start in ((a, b) for a in near for b in near):
+        a, b = start
+        for _ in range(4):
+            if abs(a) + abs(b) == hops and (a, b) not in found:
+                found.append((a, b))
+            a, b = (-b if b != SIDE // 2 else b), a
+    return found
 
 
 def lower_half(shape):
@@ -36,8 +49,8 @@
 
 def exchange_kernel(
     rows_hbm, cols_hbm, tiles, coeff_hbm, got, pair_got,
-    rows, cols, coeff, raw, turned, send, halves, blocks, near, part, part_got, mid,
-    ready, small_sems, load_sems, near_send, near_recv, main_send, main_recv, col_send, col_recv, row_send, row_recv, own_sems,
+    rows, cols, coeff, raw, turned, send, halves, blocks, near, part, part_got, mid, col_row, col_rows,
+    circles, small_sems, load_sems, near_send, near_recv, main_send, main_recv, col_send, col_recv, row_send, row_recv, list_send, list_recv, own_sems,
 ):
     aux, me = lax.axis_index("aux"), lax.axis_index("ao")
     y, z = me // SIDE, me % SIDE
@@ -54,11 +67,20 @@
     for load in loads:
         load.start()
 
-    @pl.loop(1, SIDE)
-    def _(k):
-        pl.semaphore_signal(barrier, inc=1, device_id=(aux, y * SIDE + (z + k) % SIDE), device_id_type=MESH)
-        pl.semaphore_signal(barrier, inc=1, device_id=(aux, (y + k) % SIDE * SIDE + z), device_id_type=MESH)
-
+    def beside(dy, dz):
+        return (y + dy + SIDE) % SIDE * SIDE + (z + dz + SIDE) % SIDE
+
+    def tell(semaphore):
+        for offset in offsets_at(1):
+            pl.semaphore_signal(semaphore, inc=1, device_id=(aux, beside(*offset)), device_id_type=MESH)
+
+    def widen(circle):
+        if circle > 1:
+            pl.semaphore_wait(circles.at[circle - 1], 4)
+        if circle < REACH:
+            tell(circles.at[circle])
+
+    tell(barrier)
     for shift in (1, NAO - 1):
         pl.semaphore_signal(barrier, inc=1, device_id=(aux, (me + shift) % NAO), device_id_type=MESH)
 
@@ -102,29 +124,26 @@
                 halves[2 * g + sub, pl.ds(q * OCC, OCC), :] = hq
                 send[pl.ds(QD * q, QD), g, pl.ds(8 * sub, 8), :] = hq.reshape(SIDE, 8, LANES)
         if g == 0:
-            pl.semaphore_wait(barrier, 2 * SIDE)
+            pl.semaphore_wait(barrier, 6)
             for copy in near_copies:
                 copy.start()
-
-            @pl.loop(1, SIDE)
-            def _(k):
-                pl.semaphore_signal(
-                    ready.at[SIDE - k], inc=1, device_id=(aux, y * SIDE + (z + k) % SIDE), device_id_type=MESH
-                )
+        if g < 2:
+            widen(g + 1)
 
     own = pltpu.make_async_copy(send.at[me], got.at[me], own_sems.at[0])
     own.start()
 
-    def ship(dy, dz):
-        to = (y + dy) % SIDE * SIDE + (z + dz) % SIDE
-        pltpu.make_async_remote_copy(
-            send.at[to], got.at[me], main_send, main_recv, device_id=(aux, to), device_id_type=MESH
-        ).start()
-
-    @pl.loop(1, SIDE)
-    def _(k):
-        ship(k, 0)
-        ship(0, k)
+    def ship_circle(hops):
+        if hops > 2:
+            widen(hops)
+        for offset in offsets_at(hops):
+            to = beside(*offset)
+            pltpu.make_async_remote_copy(
+                send.at[to], got.at[me], main_send, main_recv, device_id=(aux, to), device_id_type=MESH
+            ).start()
+
+    for hops in range(1, 5):
+        ship_circle(hops)
 
     for copy in near_copies:
         copy.wait()
@@ -140,16 +159,18 @@
         )
     high = total.astype(jnp.bfloat16)
     rest = (total - high.astype(jnp.float32)).astype(jnp.bfloat16)
-    part[:, pl.ds(0, OCC), :] = jnp.where(lower_half(high.shape), high, rest).reshape(QD, OCC, LANES)
-    lane = lax.broadcasted_iota(jnp.int32, (16, LANES), 1)
-    columns = jnp.zeros((16, LANES), jnp.float32)
+    part[...] = jnp.where(lower_half(high.shape), high, rest).reshape(QD, OCC, LANES)
+    lane = lax.broadcasted_iota(jnp.int32, (1, LANES), 1)
+    columns = jnp.zeros((1, LANES), jnp.float32)
     for t in range(NT):
-        columns = jnp.where(lane == 16 * z + t, jnp.maximum(cols[0, t], 0).astype(jnp.float32), columns)
-    for q in range(QD):
-        part[q, pl.ds(OCC, 16), :] = columns.astype(jnp.bfloat16)
+        here = lane == SB + 16 * (z % 4) + t
+        columns = jnp.where(here, jnp.maximum(cols[0, t], 0).astype(jnp.float32), columns)
+    col_row[...] = columns
 
     own_part = pltpu.make_async_copy(part.at[y], part_got.at[y], own_sems.at[1])
     own_part.start()
+    own_row = pltpu.make_async_copy(col_row, col_rows.at[y], own_sems.at[3])
+    own_row.start()
 
     @pl.loop(1, SIDE)
     def _(k):
@@ -157,29 +178,28 @@
         pltpu.make_async_remote_copy(
             part.at[to], part_got.at[y], col_send, col_recv, device_id=(aux, to * SIDE + z), device_id_type=MESH
         ).start()
-
-    @pl.loop(1, SIDE)
-    def _(k):
-        pl.semaphore_wait(ready.at[k], 1)
-
-        @pl.loop(1, SIDE)
-        def _(j):
-            ship(j, k)
+        pltpu.make_async_remote_copy(
+            col_row, col_rows.at[y], list_send, list_recv, device_id=(aux, to * SIDE + z), device_id_type=MESH
+        ).start()
+
+    for hops in range(5, 7):
+        ship_circle(hops)
 
     seven = pl.ds(0, SIDE - 1)
     own_part.wait()
     pltpu.make_async_copy(part_got.at[seven], part_got.at[seven], col_recv).wait()
-    arrived = part_got[0].astype(jnp.float32)
-    summed, columns = arrived[:OCC], arrived[OCC : OCC + 8]
-    row = lax.broadcasted_iota(jnp.int32, columns.shape, 0)
+    own_row.wait()
+    pltpu.make_async_copy(col_rows.at[seven], col_rows.at[seven], list_recv).wait()
+    summed = part_got[0].astype(jnp.float32)
     for k in range(1, SIDE):
-        arrived = part_got[k].astype(jnp.float32)
-        summed += arrived[:OCC]
-        columns = jnp.where(row == k, arrived[OCC : OCC + 8], columns)
+        summed += part_got[k].astype(jnp.float32)
     summed += swap_halves(summed)
-    mid[:, pl.ds(0, 8), :] = summed.reshape(SIDE, 8, LANES)
+    row = lax.broadcasted_iota(jnp.int32, (8, LANES), 0)
+    columns = jnp.zeros((8, LANES), jnp.float32)
     for k in range(SIDE):
-        mid[k, pl.ds(8, 8), :] = columns
+        columns = jnp.where(row == k, col_rows[k], columns)
+    for k in range(SIDE):
+        mid[k] = jnp.where(lower_half((8, LANES)), summed[8 * k : 8 * k + 8], columns)
     own_mid = pltpu.make_async_copy(mid.at[z], pair_got.at[z], own_sems.at[2])
     own_mid.start()
 
@@ -190,10 +210,14 @@
             mid.at[to], pair_got.at[z], row_send, row_recv, device_id=(aux, y * SIDE + to), device_id_type=MESH
         ).start()
 
+    for hops in range(7, REACH + 1):
+        ship_circle(hops)
+
     own.wait()
     own_mid.wait()
     most = pl.ds(0, NAO - 1)
     pltpu.make_async_copy(part.at[seven], part.at[seven], col_send).wait()
+    pltpu.make_async_copy(col_rows.at[seven], col_rows.at[seven], list_send).wait()
     pltpu.make_async_copy(mid.at[seven], mid.at[seven], row_send).wait()
     pltpu.make_async_copy(send.at[most], send.at[most], main_send).wait()
     pltpu.make_async_copy(pair_got.at[seven], pair_got.at[seven], row_recv).wait()
@@ -208,7 +232,7 @@
         exchange_kernel,
         out_shape=(
             jax.ShapeDtypeStruct((NAO, 3, 16, LANES), bf16),
-            jax.ShapeDtypeStruct((SIDE, 16, LANES), f32),
+            jax.ShapeDtypeStruct((SIDE, 8, LANES), f32),
         ),
         in_specs=[hbm, hbm, hbm, hbm],
         out_specs=(vmem, vmem),
@@ -222,10 +246,12 @@
             pltpu.VMEM((NT // 2, QD * OCC, LANES), bf16),
             pltpu.VMEM((3 * NB, OCC, LANES), bf16),
             pltpu.VMEM((2, OCC, NB * SB), bf16),
-            pltpu.VMEM((QD, OCC + 16, LANES), bf16),
-            pltpu.VMEM((SIDE, OCC + 16, LANES), bf16),
-            pltpu.VMEM((SIDE, 16, LANES), f32),
-            pltpu.SemaphoreType.REGULAR((SIDE,)), dma((3,)), dma((3,)), dma((2,)), dma((2,)), dma, dma, dma, dma, dma, dma, dma((3,)),
+            pltpu.VMEM((QD, OCC, LANES), bf16),
+            pltpu.VMEM((SIDE, OCC, LANES), bf16),
+            pltpu.VMEM((SIDE, 8, LANES), f32),
+            pltpu.VMEM((1, LANES), f32),
+            pltpu.VMEM((SIDE, 1, LANES), f32),
+            pltpu.SemaphoreType.REGULAR((SIDE,)), dma((3,)), dma((3,)), dma((2,)), dma((2,)), dma, dma, dma, dma, dma, dma, dma, dma, dma((4,)),
         ],
         compiler_params=pltpu.CompilerParams(collective_id=0, has_side_effects=True, vmem_limit_bytes=40 << 20),
         cost_estimate=pl.CostEstimate(flops=200_000_000, bytes_accessed=3_000_000, transcendentals=0),
@@ -233,48 +259,48 @@
     )(rows, cols, tiles, coeff)
 
 
-def place_kernel(got, pair_got, relaid, pair_ints, cols_vmem, cols, cols_sem, *sums):
+def place_kernel(got, pair_got, relaid, pair_ints, rows_vmem, rows, rows_sem, *sums):
     per = NAO // GROUPS
-    tiles_per = NB // 2
-    zero = jnp.zeros((8, LANES), jnp.float32)
-    columns = pair_got[0, pl.ds(8, 8), :]
-    for k in range(1, SIDE):
-        columns += pair_got[k, pl.ds(8, 8), :]
-    cols_vmem[...] = columns.astype(jnp.int32)
-    fetch = pltpu.make_async_copy(cols_vmem, cols, cols_sem)
+    low = lower_half((8, LANES))
+    total, later = pair_got[0], pair_got[SIDE // 2]
+    for k in range(1, SIDE // 2):
+        total += pair_got[k]
+        later += pair_got[SIDE // 2 + k]
+    source = lax.broadcasted_iota(jnp.int32, (8, LANES), 1) // 16
+    rows_vmem[...] = 8 * (jnp.where(low, swap_halves(total), later).astype(jnp.int32) + NB * source)
+    fetch = pltpu.make_async_copy(rows_vmem, rows, rows_sem)
     fetch.start()
-    for total in sums:
-        total[...] = jnp.zeros(total.shape, jnp.float32)
-    half_of = lax.broadcasted_iota(jnp.int32, (8, LANES), 1) // SB
-    low = half_of == 0
+    pair_ints[...] = (total + later)[:, :OCC]
+    for part in sums:
+        part[...] = jnp.zeros(part.shape, jnp.float32)
     fetch.wait()
 
     @pl.loop(0, per)
     def _(k):
         for s in range(NT // 2):
             for g in range(GROUPS):
-                p = g * per + k
-                v = got[p, s // 2, pl.ds(8 * (s % 2), 8), :].astype(jnp.float32)
-                w = swap_halves(v)
+                v = got[g * per + k, s // 2, pl.ds(8 * (s % 2), 8), :].astype(jnp.float32)
                 for side in range(2):
-                    both = jnp.where(low, v, w) if side == 0 else jnp.where(low, w, v)
-                    c = cols[g, 16 * k + 2 * s + side]
-                    at = tiles_per * k + lax.shift_right_logical(c, 1)
-                    sums[g][at] += jnp.where(half_of == jnp.bitwise_and(c, 1), both, zero)
-
-    for tile in range(NAO * tiles_per):
-        g, local = divmod(tile, per * tiles_per)
-        value = sums[g][local + tiles_per]
-        if local < tiles_per and g > 0:
-            value += sums[g - 1][local + (per + 1) * tiles_per]
-        if local >= (per - 1) * tiles_per and g < GROUPS - 1:
-            value += sums[g + 1][local - (per - 1) * tiles_per]
+                    at = pl.ds(pl.multiple_of(rows[g, 16 * k + 2 * s + side], 8), 8)
+                    sums[g][at, :] += jnp.where(low, v, 0.0) if side == 0 else jnp.where(low, 0.0, v)
+
+    def block(b):
+        g, local = divmod(b, per * NB)
+
+        def at(i):
+            return pl.ds(8 * i, 8)
+
+        value = sums[g][at(local + NB), :]
+        if local < NB and g > 0:
+            value += sums[g - 1][at(local + (per + 1) * NB), :]
+        if local >= (per - 1) * NB and g < GROUPS - 1:
+            value += sums[g + 1][at(local - (per - 1) * NB), :]
+        return value
+
+    for tile in range(NAO * NB // 2):
+        a, b = block(2 * tile), block(2 * tile + 1)
+        value = jnp.where(low, a, b) + swap_halves(jnp.where(low, b, a))
         relaid[:, tile * LANES : (tile + 1) * LANES] = value.astype(jnp.bfloat16)
-
-    total = pair_got[0, pl.ds(0, 8), :]
-    for k in range(1, SIDE):
-        total += pair_got[k, pl.ds(0, 8), :]
-    pair_ints[...] = total[:, :OCC]
 
 
 def place(got, pair_got):
@@ -292,7 +318,7 @@
             pltpu.VMEM((SIDE, LANES), jnp.int32),
             pltpu.SMEM((SIDE, LANES), jnp.int32),
             pltpu.SemaphoreType.DMA,
-            *[pltpu.VMEM(((per + 2) * NB // 2, 8, LANES), jnp.float32)] * GROUPS,
+            *[pltpu.VMEM(((per + 2) * NB * 8, LANES), jnp.float32)] * GROUPS,
         ],
         compiler_params=pltpu.CompilerParams(vmem_limit_bytes=40 << 20),
         cost_estimate=pl.CostEstimate(flops=1_000_000, bytes_accessed=1_500_000, transcendentals=0),

time: 49.7 us -> 42.2 us (0.85)
  Pallas kernels: 48.8 us -> 41.1 us
    pallas_call x1, Pallas kernels: 45 us -> 38 us  [exchange(): pl.pallas_call(exchange_kernel, out_shape=(jax.ShapeDtypeStruct((NAO, 3,...]
    pallas_call x1, Pallas kernels: 3.73 us -> 3.08 us  [place(): pl.pallas_call(place_kernel, out_shape=(jax.ShapeDtypeStruct((8, NAO * NB...]
where the time goes in v4:
time: 42.2 us; the launch traced here: 41.7 us
  Pallas kernels  41.1 us (97%)
  between operations  0.64 us (2%)
    pallas_call x1, Pallas kernels, exchange(): pl.pallas_call(exchange_kernel, out_shape=(jax.ShapeDtypeStruct((NAO, 3,...  38 us
    pallas_call x1, Pallas kernels, place(): pl.pallas_call(place_kernel, out_shape=(jax.ShapeDtypeStruct((8, NAO * NB...  3.08 us

profile of v4, /device:TPU:6, one launch (start us, length us, event | category | flops | bytes accessed | tf_op | source)
XLA Modules:
  0.0 41.7 jit_solution(3278651189298800631)
XLA Ops:
  0.6 38.0 %half_transform_exchange.1 = (bf16[64,3,16,128]{3,2,1,0:T(8,128)(2,1)S(1)}, f32[8,8,128]{2,1,0:T(8,128)S(1)}) custom-call(s32[1,12]{1,0:T(1,128)} %rows_hbm.1, s32[1,12]{1,0:T(1,128)} %cols_hbm.1, bf16[12,8,4096]{2,1,0:T(8,128)(2,1)} %bitcast.2, bf16[64,640]{1,0:T(8,128)(2,1)} %bitcast.3), custom_call_target="tpu_custom_call" | custom-call | flops 200000000 | bytes 3000000 | tf_op jit(solution)/shard_map/half_transform_exchange/pallas_call | solution.py:231
  38.6 3.1 %place.1 = (bf16[8,40960]{1,0:T(8,128)(2,1)}, f32[8,64]{1,0:T(8,128)}) custom-call(bf16[64,3,16,128]{3,2,1,0:T(8,128)(2,1)S(1)} %get-tuple-element.4.got, f32[8,8,128]{2,1,0:T(8,128)S(1)} %get-tuple-element.5.pair_got), custom_call_target="tpu_custom_call" | custom-call | flops 1000000 | bytes 1500000 | tf_op jit(solution)/shard_map/place/pallas_call | solution.py:309

commit v5 on v4

--- a/solution.py
+++ b/solution.py
@@ -15,19 +15,7 @@
 LANES = 128
 GROUPS = SIDE
 MESH = pl.DeviceIdType.MESH
-REACH = SIDE
-
-
-def offsets_at(hops):
-    near = range(1 - SIDE // 2, SIDE // 2 + 1)
-    found = []
-    for start in ((a, b) for a in near for b in near):
-        a, b = start
-        for _ in range(4):
-            if abs(a) + abs(b) == hops and (a, b) not in found:
-                found.append((a, b))
-            a, b = (-b if b != SIDE // 2 else b), a
-    return found
+FAR_FIRST = (4, 3, -3, 2, -2, 1, -1)
 
 
 def lower_half(shape):
@@ -50,7 +38,7 @@
 def exchange_kernel(
     rows_hbm, cols_hbm, tiles, coeff_hbm, got, pair_got,
     rows, cols, coeff, raw, turned, send, halves, blocks, near, part, part_got, mid, col_row, col_rows,
-    circles, small_sems, load_sems, near_send, near_recv, main_send, main_recv, col_send, col_recv, row_send, row_recv, list_send, list_recv, own_sems,
+    ready, small_sems, load_sems, near_send, near_recv, main_send, main_recv, col_send, col_recv, row_send, row_recv, list_send, list_recv, own_sems,
 ):
     aux, me = lax.axis_index("aux"), lax.axis_index("ao")
     y, z = me // SIDE, me % SIDE
@@ -67,20 +55,11 @@
     for load in loads:
         load.start()
 
-    def beside(dy, dz):
-        return (y + dy + SIDE) % SIDE * SIDE + (z + dz + SIDE) % SIDE
-
-    def tell(semaphore):
-        for offset in offsets_at(1):
-            pl.semaphore_signal(semaphore, inc=1, device_id=(aux, beside(*offset)), device_id_type=MESH)
-
-    def widen(circle):
-        if circle > 1:
-            pl.semaphore_wait(circles.at[circle - 1], 4)
-        if circle < REACH:
-            tell(circles.at[circle])
-
-    tell(barrier)
+    @pl.loop(1, SIDE)
+    def _(k):
+        pl.semaphore_signal(barrier, inc=1, device_id=(aux, y * SIDE + (z + k) % SIDE), device_id_type=MESH)
+        pl.semaphore_signal(barrier, inc=1, device_id=(aux, (y + k) % SIDE * SIDE + z), device_id_type=MESH)
+
     for shift in (1, NAO - 1):
         pl.semaphore_signal(barrier, inc=1, device_id=(aux, (me + shift) % NAO), device_id_type=MESH)
 
@@ -124,26 +103,36 @@
                 halves[2 * g + sub, pl.ds(q * OCC, OCC), :] = hq
                 send[pl.ds(QD * q, QD), g, pl.ds(8 * sub, 8), :] = hq.reshape(SIDE, 8, LANES)
         if g == 0:
-            pl.semaphore_wait(barrier, 6)
+            pl.semaphore_wait(barrier, 2 * SIDE)
             for copy in near_copies:
                 copy.start()
-        if g < 2:
-            widen(g + 1)
+
+            @pl.loop(1, SIDE)
+            def _(k):
+                pl.semaphore_signal(
+                    ready.at[SIDE - k], inc=1, device_id=(aux, y * SIDE + (z + k) % SIDE), device_id_type=MESH
+                )
 
     own = pltpu.make_async_copy(send.at[me], got.at[me], own_sems.at[0])
     own.start()
 
-    def ship_circle(hops):
-        if hops > 2:
-            widen(hops)
-        for offset in offsets_at(hops):
-            to = beside(*offset)
-            pltpu.make_async_remote_copy(
-                send.at[to], got.at[me], main_send, main_recv, device_id=(aux, to), device_id_type=MESH
-            ).start()
-
-    for hops in range(1, 5):
-        ship_circle(hops)
+    def ship(dy, dz):
+        to = (y + dy + SIDE) % SIDE * SIDE + (z + dz + SIDE) % SIDE
+        pltpu.make_async_remote_copy(
+            send.at[to], got.at[me], main_send, main_recv, device_id=(aux, to), device_id_type=MESH
+        ).start()
+
+    for far in FAR_FIRST:
+        ship(far, 0)
+        ship(0, far)
+
+    def ship_column(k):
+        pl.semaphore_wait(ready.at[k % SIDE], 1)
+        for j in FAR_FIRST:
+            ship(j, k)
+
+    for k in FAR_FIRST[:1]:
+        ship_column(k)
 
     for copy in near_copies:
         copy.wait()
@@ -182,8 +171,8 @@
             col_row, col_rows.at[y], list_send, list_recv, device_id=(aux, to * SIDE + z), device_id_type=MESH
         ).start()
 
-    for hops in range(5, 7):
-        ship_circle(hops)
+    for k in FAR_FIRST[1:5]:
+        ship_column(k)
 
     seven = pl.ds(0, SIDE - 1)
     own_part.wait()
@@ -210,8 +199,8 @@
             mid.at[to], pair_got.at[z], row_send, row_recv, device_id=(aux, y * SIDE + to), device_id_type=MESH
         ).start()
 
-    for hops in range(7, REACH + 1):
-        ship_circle(hops)
+    for k in FAR_FIRST[5:]:
+        ship_column(k)
 
     own.wait()
     own_mid.wait()

time: 42.2 us -> 41.6 us (0.986)
  no operation moved by 1% of the time
where the time goes in v5:
time: 41.6 us; the launch traced here: 41.4 us
  Pallas kernels  40.8 us (98%)
  between operations  0.64 us (2%)
    pallas_call x1, Pallas kernels, exchange(): pl.pallas_call(exchange_kernel, out_shape=(jax.ShapeDtypeStruct((NAO, 3,...  37.7 us
    pallas_call x1, Pallas kernels, place(): pl.pallas_call(place_kernel, out_shape=(jax.ShapeDtypeStruct((8, NAO * NB...  3.08 us

profile of v5, /device:TPU:6, one launch (start us, length us, event | category | flops | bytes accessed | tf_op | source)
XLA Modules:
  0.0 41.4 jit_solution(15055024397580651851)
XLA Ops:
  0.6 37.7 %half_transform_exchange.1 = (bf16[64,3,16,128]{3,2,1,0:T(8,128)(2,1)S(1)}, f32[8,8,128]{2,1,0:T(8,128)S(1)}) custom-call(s32[1,12]{1,0:T(1,128)} %rows_hbm.1, s32[1,12]{1,0:T(1,128)} %cols_hbm.1, bf16[12,8,4096]{2,1,0:T(8,128)(2,1)} %bitcast.2, bf16[64,640]{1,0:T(8,128)(2,1)} %bitcast.3), custom_call_target="tpu_custom_call" | custom-call | flops 200000000 | bytes 3000000 | tf_op jit(solution)/shard_map/half_transform_exchange/pallas_call | solution.py:220
  38.3 3.1 %place.1 = (bf16[8,40960]{1,0:T(8,128)(2,1)}, f32[8,64]{1,0:T(8,128)}) custom-call(bf16[64,3,16,128]{3,2,1,0:T(8,128)(2,1)S(1)} %get-tuple-element.4.got, f32[8,8,128]{2,1,0:T(8,128)S(1)} %get-tuple-element.5.pair_got), custom_call_target="tpu_custom_call" | custom-call | flops 1000000 | bytes 1500000 | tf_op jit(solution)/shard_map/place/pallas_call | solution.py:298
